TPU v7x, 512 devices: a whole 4x8x8 slice. The times are simulated.
512 devices in a mesh: head: 8 (over z_hi, core), ctx: 64 (over z_lo, y, x).
Axes of the slice: x: 4, y: 8, z: 8 (z_hi: 4, z_lo: 2; z = z_hi * 2 + z_lo), core: 2. Of those that a mesh axis runs over, the one named last changes fastest.
Arguments:
- queries: bfloat16 [8192, 3072], P(('head', 'ctx')), may hold values from -15 to 15
- keys: bfloat16 [8192, 3072], P(('head', 'ctx')), may hold values from -6 to 6
- values: bfloat16 [8192, 3072], P(('head', 'ctx')), may hold values from -6 to 6
- d_queries: bfloat16 [8192, 3072], P(('head', 'ctx')), may hold values from -6 to 6
- d_keys: bfloat16 [8192, 3072], P(('head', 'ctx')), may hold values from -6 to 6
- d_values: bfloat16 [8192, 3072], P(('head', 'ctx')), may hold values from -6 to 6
Outputs:
- attended: bfloat16 [8192, 3072], P(('head', 'ctx'))
- d_attended: bfloat16 [8192, 3072], P(('head', 'ctx'))
All inputs are finite; a program needn't handle non-finite values.
Results may differ from a plain program's by a relative error of at most 0.035.
Values may be sent and summed in bfloat16 or wider, within the bound.
A program may use at most 128 MiB of HBM per device.

v0:
```python
import jax
import jax.numpy as jnp
from jax import lax
from jax.sharding import PartitionSpec as P

HD = 128


def make_step(query_cols, dquery_cols):
    row_count = query_cols.shape[0]
    head_count = query_cols.shape[1] // HD
    score_scale = HD ** (-0.5)
    query_three = query_cols.reshape(row_count, head_count, HD)
    joined_query = jnp.concatenate(
        [dquery_cols.reshape(row_count, head_count, HD), query_three], axis=2
    )

    def split_heads(tensor):
        return tensor.reshape(tensor.shape[0], head_count, HD)

    def joint_step(running, pieces, offset):
        row_peak, row_total, primal_acc, tangent_acc, weighted = running
        key_block, value_block, dkey_block, dvalue_block = pieces
        key_three = split_heads(key_block)
        scores = (
            jnp.einsum("rhd,nhd->hrn", query_three, key_three, preferred_element_type=jnp.float32)
            * score_scale
        )
        joined_key = jnp.concatenate([key_three, split_heads(dkey_block)], axis=2)
        d_scores = (
            jnp.einsum("rhd,nhd->hrn", joined_query, joined_key, preferred_element_type=jnp.float32)
            * score_scale
        )
        new_peak = jnp.maximum(row_peak, jnp.max(scores, axis=2))
        factor = jnp.exp(row_peak - new_peak)
        weights = jnp.exp(scores - new_peak[..., None])
        weights_bf = weights.astype(jnp.bfloat16)
        tangent_mix = weights * d_scores
        mix_bf = tangent_mix.astype(jnp.bfloat16)
        value_three = split_heads(value_block)
        primal_part = jnp.einsum(
            "hrn,nhd->hrd", weights_bf, value_three, preferred_element_type=jnp.float32
        )
        joined_weights = jnp.concatenate([mix_bf, weights_bf], axis=2)
        stacked = jnp.concatenate([value_three, split_heads(dvalue_block)], axis=0)
        tangent_part = jnp.einsum(
            "hrn,nhd->hrd", joined_weights, stacked, preferred_element_type=jnp.float32
        )
        row_total = jnp.sum(weights, axis=2)
        primal_acc = primal_part
        tangent_acc = tangent_part
        weighted = jnp.sum(tangent_mix, axis=2)
        return (new_peak, row_total, primal_acc, tangent_acc, weighted)

    peak_init = jnp.full((head_count, row_count), -1e30, jnp.float32)
    zero_rows = jnp.zeros((head_count, row_count), jnp.float32)
    zero_block = jnp.zeros((head_count, row_count, HD), jnp.float32)
    return (joint_step, (peak_init, zero_rows, zero_block, zero_block, zero_rows))


def finish(state):
    row_peak, row_total, primal_acc, tangent_acc, weighted = state
    primal_out = primal_acc / row_total[..., None]
    row_mean = weighted / row_total
    tangent_out = tangent_acc / row_total[..., None] - primal_out * row_mean[..., None]
    return (primal_out, tangent_out)


def on_device(queries, keys, values, d_queries, d_keys, d_values):
    query_loc, key_loc, value_loc, dquery_loc, dkey_loc, dvalue_loc = (
        lax.all_to_all(queries, "head", split_axis=1, concat_axis=0, tiled=True),
        lax.all_to_all(keys, "head", split_axis=1, concat_axis=0, tiled=True),
        lax.all_to_all(values, "head", split_axis=1, concat_axis=0, tiled=True),
        lax.all_to_all(d_queries, "head", split_axis=1, concat_axis=0, tiled=True),
        lax.all_to_all(d_keys, "head", split_axis=1, concat_axis=0, tiled=True),
        lax.all_to_all(d_values, "head", split_axis=1, concat_axis=0, tiled=True),
    )
    row_count = query_loc.shape[0]
    head_count = query_loc.shape[1] // HD
    step_fn, init_state = make_step(query_loc, dquery_loc)
    state = step_fn(
        init_state,
        (
            lax.all_gather(key_loc, "ctx", axis=0, tiled=True),
            lax.all_gather(value_loc, "ctx", axis=0, tiled=True),
            lax.all_gather(dkey_loc, "ctx", axis=0, tiled=True),
            lax.all_gather(dvalue_loc, "ctx", axis=0, tiled=True),
        ),
        jnp.int32(0),
    )
    primal_out, tangent_out = finish(state)
    primal_rows = (
        primal_out.transpose(1, 0, 2).reshape(row_count, head_count * HD).astype(jnp.bfloat16)
    )
    tangent_rows = (
        tangent_out.transpose(1, 0, 2).reshape(row_count, head_count * HD).astype(jnp.bfloat16)
    )
    attended, d_attended = (
        lax.all_to_all(primal_rows, "head", split_axis=0, concat_axis=1, tiled=True),
        lax.all_to_all(tangent_rows, "head", split_axis=0, concat_axis=1, tiled=True),
    )
    return (attended, d_attended)


def solution(mesh):
    in_specs = (
        P(("head", "ctx"), None),
        P(("head", "ctx"), None),
        P(("head", "ctx"), None),
        P(("head", "ctx"), None),
        P(("head", "ctx"), None),
        P(("head", "ctx"), None),
    )
    out_specs = (P(("head", "ctx"), None), P(("head", "ctx"), None))
    return jax.shard_map(
        on_device, mesh=mesh, in_specs=in_specs, out_specs=out_specs, check_vma=False
    )
```

profile of v0, /device:TPU:1, one launch (start us, length us, event | category | flops | bytes accessed | tf_op | source)
XLA Modules:
  0.0 1356.5 jit_solution(17032157169654188834)
XLA Ops:
  7.2 0.0 all-gather.5.cloned.1.call-start
  7.2 0.9 copy.91
  8.1 19.9 %all_to_all.140 = bf16[16,8,384]{2,0,1:T(8,128)(2,1)} all-to-all(bf16[16,8,384]{2,0,1:T(8,128)(2,1)S(1)} %bitcast.84), channel_id=1, replica_groups=mesh['head'=8,'ctx'=64] {'head'}, dimensions={1} | all-to-all | bytes 196608 | tf_op jit(solution)/shard_map/all_to_all | solution.py:72
  28.0 0.0 all-gather.5.cloned.1.call-update
  28.0 0.0 all-gather.9.cloned.1.call-start
  28.0 0.9 copy.88
  29.0 11.9 all_to_all.141
  40.8 0.0 all-gather.7.cloned.1.call-start
  40.9 0.9 copy.90
  41.8 12.0 all_to_all.142
  53.9 0.0 all-gather.11.cloned.1.call-start
  53.9 0.9 copy.87
  54.8 12.3 all_to_all.143
  67.2 1.5 copy.92
  68.7 4.2 all-to-all-start
  72.9 1.5 copy.89
  74.5 6.6 all-to-all-done
  81.1 4.1 all-to-all-start.4
  85.2 7.7 all-to-all-done.4
  93.0 199.2 %all-gather.5.cloned.1.call-done = bf16[8192,384]{1,0:T(8,128)(2,1)} async-done(((bf16[128,384]{1,0:T(8,128)(2,1)}), bf16[8192,384]{1,0:T(8,128)(2,1)}) %all-gather.5.cloned.1.call-update) | async-done | bytes 6291472 | tf_op jit(solution)/shard_map/all_gather | solution.py:84
  292.1 8.8 copy.50
  300.9 8.6 copy.63
  309.5 293.8 %all-gather.9.cloned.1.call-done = bf16[8192,384]{1,0:T(8,128)(2,1)} async-done(((bf16[128,384]{1,0:T(8,128)(2,1)}), bf16[8192,384]{1,0:T(8,128)(2,1)}) %all-gather.9.cloned.1.call-update) | async-done | bytes 6291472 | tf_op jit(solution)/shard_map/all_gather | solution.py:86
  603.4 8.7 copy.62
  612.0 8.6 copy.64
  620.6 292.9 %all-gather.7.cloned.1.call-done = bf16[8192,384]{1,0:T(8,128)(2,1)} async-done(((bf16[128,384]{1,0:T(8,128)(2,1)}), bf16[8192,384]{1,0:T(8,128)(2,1)}) %all-gather.7.cloned.1.call-update) | async-done | bytes 6291472 | tf_op jit(solution)/shard_map/all_gather | solution.py:85
  913.5 8.7 copy.54
  922.2 8.6 copy.67
  930.8 9.1 fusion.42
  940.0 283.4 %all-gather.11.cloned.1.call-done = bf16[8192,384]{1,0:T(8,128)(2,1)} async-done(((bf16[128,384]{1,0:T(8,128)(2,1)}), bf16[8192,384]{1,0:T(8,128)(2,1)}) %all-gather.11.cloned.1.call-update) | async-done | bytes 6291472 | tf_op jit(solution)/shard_map/all_gather | solution.py:87
  1223.4 8.8 copy.66
  1232.2 8.6 copy.68
  1240.8 10.0 fusion.13
  1250.8 13.1 fusion.41
  1263.9 6.5 fusion.43
  1270.5 1.1 copy-done
  1271.5 0.6 slice-done.1
  1272.1 7.0 fusion.31
  1279.2 0.1 copy.69
  1279.3 0.7 convert_element_type.25
  1280.0 49.5 %all-to-all-start.7 = ((bf16[8,16,384]{2,1,0:T(8,128)(2,1)}), bf16[8,16,384]{2,1,0:T(8,128)(2,1)S(1)}, u32[]{:S(2)}, u32[]{:S(2)}) async-start(bf16[8,16,384]{2,1,0:T(8,128)(2,1)} %convert_element_type.25), calls=%async_computation.7 | async-start | bytes 196608 | tf_op jit(solution)/shard_map/all_to_all | solution.py:100
  1329.6 0.1 copy.56
  1329.6 0.7 convert_element_type.22
  1330.4 6.8 all-to-all-done.7
  1337.2 4.4 all-to-all-start.3
  1341.6 0.7 copy.80
  1342.3 7.1 all-to-all-done.3
  1349.4 0.7 copy.79
  (14 shorter events, 0.2 us)
Async XLA Ops:
  7.2 285.0 %all-gather.5.cloned.1.call-start = ((), (), s32[]{:S(2)}) async-start(), calls=%async_computation.8 | async-start | bytes 6389760 | tf_op jit(solution)/shard_map/all_gather | solution.py:84
  28.0 575.4 %all-gather.9.cloned.1.call-start = ((), (), s32[]{:S(2)}) async-start(), calls=%async_computation.10 | async-start | bytes 6389760 | tf_op jit(solution)/shard_map/all_gather | solution.py:86
  40.8 872.6 %all-gather.7.cloned.1.call-start = ((), (), s32[]{:S(2)}) async-start(), calls=%async_computation.9 | async-start | bytes 6389760 | tf_op jit(solution)/shard_map/all_gather | solution.py:85
  53.9 1169.6 %all-gather.11.cloned.1.call-start = ((), (), s32[]{:S(2)}) async-start(), calls=%async_computation.11 | async-start | bytes 6389760 | tf_op jit(solution)/shard_map/all_gather | solution.py:87
  68.7 12.4 all-to-all-start
  81.1 11.9 all-to-all-start.4
  1263.9 6.6 slice-start
  1263.9 7.7 copy-start
  1263.9 8.3 slice-start.1
  1280.0 57.2 %all-to-all-start.7 = ((bf16[8,16,384]{2,1,0:T(8,128)(2,1)}), bf16[8,16,384]{2,1,0:T(8,128)(2,1)S(1)}, u32[]{:S(2)}, u32[]{:S(2)}) async-start(bf16[8,16,384]{2,1,0:T(8,128)(2,1)} %convert_element_type.25), calls=%async_computation.7 | async-start | bytes 196608 | tf_op jit(solution)/shard_map/all_to_all | solution.py:100
  1337.2 12.2 all-to-all-start.3
Sparse Core Ops, SparseCore 0:
  28.1 263.9 all-gather.4
  294.2 309.0 all-gather.8
  605.4 307.9 all-gather.6
  915.4 307.9 all-gather.10
where the time goes:
time: 1360 us
  waiting for transfers between devices  1100 us (81%)
  local copies, waits for them, and re-layouts  80.8 us (6%)
  starting transfers between devices  62.4 us (5%)
  blocking collectives  56.1 us (4%)
  matrix products  35.8 us (3%)
  between operations  13.9 us (1%)
    all_gather x1, waiting for transfers between devices, on_device(): lax.all_gather(dkey_loc, 'ctx', axis=0, tiled=True)  294 us
    all_gather x1, waiting for transfers between devices, on_device(): lax.all_gather(value_loc, 'ctx', axis=0, tiled=True)  293 us
    all_gather x1, waiting for transfers between devices, on_device(): lax.all_gather(dvalue_loc, 'ctx', axis=0, tiled=True)  283 us
    all_gather x1, waiting for transfers between devices, on_device(): lax.all_gather(key_loc, 'ctx', axis=0, tiled=True)  199 us
    all_to_all x1, starting transfers between devices, on_device(): lax.all_to_all(tangent_rows, 'head', split_axis=0, concat_axis=1, tiled=T...  49.5 us
    reshape x4, local copies, waits for them, and re-layouts, split_heads(): return tensor.reshape(tensor.shape[0], head_count, HD)  34.5 us
  transfers between devices with their start and end apart: 8, of which 8 were waited for; matrix products, arithmetic and copies ran while one was open for 5% of the time, Pallas kernels for 0%

commit v1 on v0

v1 whole, which is shorter than its diff:
```python
import functools

import jax
import jax.numpy as jnp
import numpy as np
from jax import lax
from jax.experimental import pallas as pl
from jax.experimental.pallas import tpu as pltpu
from jax.sharding import PartitionSpec as P

HD = 128
CORES = 2
SCALE = HD**-0.5
LOG2E = 1.4426950408889634
MESH = pl.DeviceIdType.MESH

DIMS = (4, 8, 8, 2)

PLANS = ("y", "z", "y")


def head_of(slot, place, dims):
    if slot == 1:
        return 2 * dims[1] + place
    return 2 * place + slot // 2


def steps_of(size):
    half = size // 2
    return {(0, 1): half, (0, -1): size - 1 - half, (1, 1): size - 1 - half, (1, -1): half}


def kernel(
    dims,
    q_ref, k_ref, v_ref, dq_ref, dk_ref, dv_ref,
    out_ref, dout_ref,
    stage, landed, kb, qb, part, stat, rpart, rstat, outgo, outcome, s_buf,
    a_send, a_recv, ring_send, ring_recv, sib_send, sib_recv, q_send, q_recv,
    p_send, p_recv, t_send, t_recv, o_send, o_recv,
):
    nx, ny, nz, zlo = dims
    tok = q_ref.shape[0]
    head, ctx = lax.axis_index("head"), lax.axis_index("ctx")
    core = head % CORES
    z = (head // CORES) * zlo + ctx // (ny * nx)
    y = (ctx // nx) % ny
    x = ctx % nx

    def dev(x, y, z, core):
        return ((z // zlo) * CORES + core, (z % zlo) * (ny * nx) + y * nx + x)

    def a_size(s):
        return ny if PLANS[s] == "y" else nz

    def r_size(s):
        return nz if PLANS[s] == "y" else ny

    def a_me(s):
        return y if PLANS[s] == "y" else z

    def r_me(s):
        return z if PLANS[s] == "y" else y

    def a_dev(s, p):
        return dev(x, p, z, core) if PLANS[s] == "y" else dev(x, y, p, core)

    def r_dev(s, r):
        return dev(x, y, r, core) if PLANS[s] == "y" else dev(x, r, z, core)

    sibling = dev(x, y, z, 1 - core)

    def remote(src, dst, ssem, rsem, to):
        return pltpu.make_async_remote_copy(
            src_ref=src, dst_ref=dst, send_sem=ssem, recv_sem=rsem,
            device_id=to, device_id_type=MESH,
        )

    def drain(ref, sem):
        pltpu.make_async_copy(ref, ref, sem).wait()

    barrier = pltpu.get_barrier_semaphore()
    peers = [sibling]
    peers += [dev(x, (y + d) % ny, z, core) for d in range(1, ny)]
    peers += [dev(x, y, (z + d) % nz, core) for d in range(1, nz)]
    peers += [dev((x + d) % nx, y, z, core) for d in range(1, nx)]
    for peer in peers:
        pl.semaphore_signal(barrier, inc=1, device_id=peer, device_id_type=MESH)

    inputs = (k_ref, dk_ref, v_ref, dv_ref, q_ref, dq_ref)
    for s in range(3):
        for p in range(a_size(s)):
            h = head_of(s, p, dims)
            for i, ref in enumerate(inputs):
                stage[s, p, i] = ref[:, h * HD : (h + 1) * HD]
    pl.semaphore_wait(barrier, len(peers))

    def scatter(s):
        n, me = a_size(s), a_me(s)
        for d in sorted(range(1, n), key=lambda d: -min(d, n - d)):
            p = (me + d) % n
            remote(stage.at[s, p], landed.at[s, me], a_send.at[s], a_recv.at[s], a_dev(s, p)).start()

    def ring_copy(s, piece, way, r, to):
        block = kb.at[s, piece, core, r]
        return remote(block, block, ring_send.at[s, piece], ring_recv.at[s, piece, r], to)

    def sib_copy(s, piece, r):
        block = kb.at[s, piece, core, r]
        return remote(block, block, sib_send.at[s, piece], sib_recv.at[s, piece], sibling)

    def begin(s):
        n, me, r, rn = a_size(s), a_me(s), r_me(s), r_size(s)
        landed[s, me] = stage[s, me]
        if n > 1:
            drain(landed.at[s, pl.ds(0, n - 1)], a_recv.at[s])
        for i in range(4):
            for p in range(n):
                kb[s, i // 2, core, r, i % 2, p * tok : (p + 1) * tok] = landed[s, p, i]
        for piece in range(2):
            for way in (1, -1):
                if steps_of(rn)[piece, way] >= 1:
                    ring_copy(s, piece, way, r, r_dev(s, (r + way) % rn)).start()
        for i in range(2):
            for p in range(n):
                qb[s, x, i, p * tok : (p + 1) * tok] = landed[s, p, 4 + i]
        for d in range(1, nx):
            mine = qb.at[s, x]
            remote(mine, mine, q_send.at[s], q_recv.at[s], dev((x + d) % nx, y, z, core)).start()
        for piece in range(2):
            sib_copy(s, piece, r).start()

    def hop(s, h):
        rn, r = r_size(s), r_me(s)
        for piece in range(2):
            for way in (1, -1):
                most = steps_of(rn)[piece, way]
                if h > most:
                    continue
                at = (r - way * h) % rn
                ring_copy(s, piece, way, at, r_dev(s, r)).wait_recv()
                if h < most:
                    ring_copy(s, piece, way, at, r_dev(s, (r + way) % rn)).start()
                sib_copy(s, piece, at).start()

    def gathered(s):
        rn = r_size(s)
        for piece in range(2):
            drain(kb.at[s, piece, 0, pl.ds(0, rn)], sib_recv.at[s, piece])
        if nx > 1:
            drain(qb.at[s, pl.ds(0, nx - 1)], q_recv.at[s])

    def attend(s, first, count):
        rows = count * 128
        rn = r_size(s)
        keys = CORES * rn * 128

        def pair(ref_at):
            return ref_at.reshape(-1, HD)

        q = pair(qb[s, first : first + count, 0])
        dq = pair(qb[s, first : first + count, 1])
        dq_q = jnp.concatenate([dq, q], axis=1)
        nt = (((1,), (1,)), ((), ()))
        step = 256
        tiles = keys // step

        def block(piece, i, j):
            c, r0 = (2 * j) // rn, (2 * j) % rn
            if rn % 2:
                raise ValueError
            return pair(kb[s, piece, c, r0 : r0 + 2, i])

        peak = None
        for j in range(tiles):
            sc = lax.dot_general(q, block(0, 0, j), nt, preferred_element_type=jnp.float32)
            s_buf[:rows, j * step : (j + 1) * step] = sc
            m = jnp.maximum(sc[:, :128], sc[:, 128:])
            peak = m if peak is None else jnp.maximum(peak, m)
        peak = jnp.max(peak, axis=1, keepdims=True) * (SCALE * LOG2E)
        total = jnp.zeros((rows, 128), jnp.float32)
        mean = jnp.zeros((rows, 128), jnp.float32)
        acc = jnp.zeros((rows, 2 * HD), jnp.float32)
        acc2 = jnp.zeros((rows, HD), jnp.float32)
        for j in range(tiles):
            k, dk, v, dv = block(0, 0, j), block(0, 1, j), block(1, 0, j), block(1, 1, j)
            w = jnp.exp2(s_buf[:rows, j * step : (j + 1) * step] * (SCALE * LOG2E) - peak)
            ds = lax.dot_general(
                dq_q, jnp.concatenate([k, dk], axis=1), nt, preferred_element_type=jnp.float32
            )
            mix = w * ds
            total += w[:, :128] + w[:, 128:]
            mean += mix[:, :128] + mix[:, 128:]
            acc += jnp.dot(
                w.astype(jnp.bfloat16), jnp.concatenate([v, dv], axis=1),
                preferred_element_type=jnp.float32,
            )
            acc2 += jnp.dot(mix.astype(jnp.bfloat16), v, preferred_element_type=jnp.float32)
        total = jnp.sum(total, axis=1, keepdims=True)
        inv = 1.0 / total
        mean = jnp.sum(mean, axis=1, keepdims=True) * (SCALE * inv)
        primal = acc[:, :HD] * inv
        tangent = (acc2 * SCALE + acc[:, HD:]) * inv - primal * mean
        lane = lax.broadcasted_iota(jnp.int32, (128, 128), 1)
        for c in range(count):
            rs = slice(c * 128, (c + 1) * 128)
            part[s, first + c, 0] = primal[rs].astype(jnp.bfloat16)
            part[s, first + c, 1] = tangent[rs].astype(jnp.bfloat16)
            wide = jnp.where(lane == 0, peak[rs], jnp.where(lane == 1, total[rs], mean[rs]))
            stat[s, first + c] = wide.T[:8]

    def share(s):
        for d in range(1, nx):
            to = (x + d) % nx
            dst = dev(to, y, z, core)
            remote(part.at[s, to], rpart.at[s, x], p_send.at[s], p_recv.at[s], dst).start()
            remote(stat.at[s, to], rstat.at[s, x], t_send.at[s], t_recv.at[s], dst).start()

    def merge(s):
        rpart[s, x] = part[s, x]
        rstat[s, x] = stat[s, x]
        if nx > 1:
            drain(rpart.at[s, pl.ds(0, nx - 1)], p_recv.at[s])
            drain(rstat.at[s, pl.ds(0, nx - 1)], t_recv.at[s])
        stats = [rstat[s, i] for i in range(nx)]
        top = functools.reduce(jnp.maximum, [t[0:1] for t in stats])
        shares = [jnp.exp2(t[0:1] - top) * t[1:2] for t in stats]
        inv = 1.0 / functools.reduce(jnp.add, shares)
        shares = [a * inv for a in shares]
        mean = functools.reduce(jnp.add, [a * t[2:3] for a, t in zip(shares, stats)])
        rows = [a for a in shares] + [a * (t[2:3] - mean) for a, t in zip(shares, stats)]
        rows.append(jnp.zeros((128 - len(rows), 128), jnp.float32))
        cols = jnp.concatenate(rows, axis=0).T
        primal = jnp.zeros((128, HD), jnp.float32)
        tangent = jnp.zeros((128, HD), jnp.float32)
        for i in range(nx):
            o = rpart[s, i, 0].astype(jnp.float32)
            primal += cols[:, i : i + 1] * o
            tangent += cols[:, i : i + 1] * rpart[s, i, 1].astype(jnp.float32) + cols[:, nx + i : nx + i + 1] * o
        primal, tangent = primal.astype(jnp.bfloat16), tangent.astype(jnp.bfloat16)
        n, me = a_size(s), a_me(s)
        for p in range(n):
            outgo[s, p, 0] = primal[p * tok : (p + 1) * tok]
            outgo[s, p, 1] = tangent[p * tok : (p + 1) * tok]
        for d in sorted(range(1, n), key=lambda d: -min(d, n - d)):
            p = (me + d) % n
            remote(outgo.at[s, p], outcome.at[s, me], o_send.at[s], o_recv.at[s], a_dev(s, p)).start()
        outcome[s, me] = outgo[s, me]

    def finish(s):
        n = a_size(s)
        if n > 1:
            drain(outcome.at[s, pl.ds(0, n - 1)], o_recv.at[s])
        for p in range(n):
            h = head_of(s, p, dims)
            out_ref[:, h * HD : (h + 1) * HD] = outcome[s, p, 0]
            dout_ref[:, h * HD : (h + 1) * HD] = outcome[s, p, 1]

    for s in range(3):
        scatter(s)
    begin(0)
    begin(1)
    last = [r_size(s) // 2 for s in range(3)]
    for h in range(1, max(last[0], last[1]) + 1):
        if h <= last[0]:
            hop(0, h)
        if h <= last[1]:
            hop(1, h)
        if h == max(last[0] - 1, 1):
            begin(2)

    half = max(nx // 2, 1)
    jobs = []
    for s in range(2):
        jobs.append(functools.partial(gathered, s))
        jobs += [functools.partial(attend, s, f, half) for f in range(0, nx, half)]
        jobs.append(functools.partial(share, s))
    per = -(-len(jobs) // last[2])
    for h in range(1, last[2] + 1):
        for job in jobs[(h - 1) * per : h * per]:
            job()
        hop(2, h)
    merge(0)
    gathered(2)
    for f in range(0, nx, half):
        attend(2, f, half)
    share(2)
    merge(1)
    merge(2)
    for s in range(3):
        finish(s)

    for s in range(3):
        n, rn = a_size(s), r_size(s)
        if n > 1:
            drain(stage.at[s, pl.ds(0, n - 1)], a_send.at[s])
            drain(outgo.at[s, pl.ds(0, n - 1)], o_send.at[s])
        for piece in range(2):
            drain(kb.at[s, piece, 0, pl.ds(0, rn)], sib_send.at[s, piece])
            drain(kb.at[s, piece, 0, pl.ds(0, rn - 1)], ring_send.at[s, piece])
        if nx > 1:
            drain(qb.at[s, pl.ds(0, nx - 1)], q_send.at[s])
            drain(part.at[s, pl.ds(0, nx - 1)], p_send.at[s])
            drain(stat.at[s, pl.ds(0, nx - 1)], t_send.at[s])


def on_device(dims, *arrays):
    nx, ny, nz, _ = dims
    tok = arrays[0].shape[0]
    na = nr = max(ny, nz)
    bf, f32 = jnp.bfloat16, jnp.float32
    dma = pltpu.SemaphoreType.DMA
    shape = jax.ShapeDtypeStruct(arrays[0].shape, bf)
    return pl.pallas_call(
        functools.partial(kernel, dims),
        out_shape=(shape, shape),
        in_specs=[pl.BlockSpec(memory_space=pltpu.VMEM)] * 6,
        out_specs=(pl.BlockSpec(memory_space=pltpu.VMEM),) * 2,
        scratch_shapes=[
            pltpu.VMEM((3, na, 6, tok, HD), bf),
            pltpu.VMEM((3, na, 6, tok, HD), bf),
            pltpu.VMEM((3, 2, CORES, nr, 2, na * tok, HD), bf),
            pltpu.VMEM((3, nx, 2, na * tok, HD), bf),
            pltpu.VMEM((3, nx, 2, 128, HD), bf),
            pltpu.VMEM((3, nx, 8, 128), f32),
            pltpu.VMEM((3, nx, 2, 128, HD), bf),
            pltpu.VMEM((3, nx, 8, 128), f32),
            pltpu.VMEM((3, na, 2, tok, HD), bf),
            pltpu.VMEM((3, na, 2, tok, HD), bf),
            pltpu.VMEM((max(nx // 2, 1) * 128, CORES * nr * 128), f32),
            dma((3,)), dma((3,)),
            dma((3, 2)), dma((3, 2, nr)),
            dma((3, 2)), dma((3, 2)),
            dma((3,)), dma((3,)),
            dma((3,)), dma((3,)),
            dma((3,)), dma((3,)),
            dma((3,)), dma((3,)),
        ],
        compiler_params=pltpu.CompilerParams(
            collective_id=0, has_side_effects=True, vmem_limit_bytes=48 * 1024 * 1024
        ),
        cost_estimate=pl.CostEstimate(flops=5 * 10**9, bytes_accessed=10**6, transcendentals=3 * 10**6),
    )(*arrays)


def solution(mesh):
    spec = P(("head", "ctx"), None)
    return jax.shard_map(
        functools.partial(on_device, DIMS),
        mesh=mesh,
        in_specs=(spec,) * 6,
        out_specs=(spec, spec),
        check_vma=False,
    )
```

time: 1360 us -> 78.9 us (0.06)
  waiting for transfers between devices: 1100 us -> 0 us
  local copies, waits for them, and re-layouts: 80.8 us -> 6.63 us
  Pallas kernels: 0 us -> 71.4 us
  starting transfers between devices: 62.4 us -> 0 us
  blocking collectives: 56.1 us -> 0 us
  matrix products: 35.8 us -> 0 us
    all_gather x4 -> x0, waiting for transfers between devices: 1070 us -> none  [the longest x1 294 us: on_device(): lax.all_gather(dkey_loc, 'ctx', axis=0, tiled=True)]
    pallas_call x0 -> x1, Pallas kernels: none -> 71.4 us  [on_device(): pl.pallas_call(functools.partial(kernel, dims), out_shape=(shape, shape),...]
    all_to_all x4 -> x0, starting transfers between devices: 62.3 us -> none  [the longest x1 49.5 us: on_device(): lax.all_to_all(tangent_rows, 'head', split_axis=0, concat_axis=1, tiled=T...]
    all_to_all x4 -> x0, blocking collectives: 56.1 us -> none  [the longest x1 19.9 us: on_device(): lax.all_to_all(keys, 'head', split_axis=1, concat_axis=0, tiled=True)]
    dot_general x4 -> x0, matrix products: 35.8 us -> none  [the longest x1 13.1 us: joint_step(): jnp.einsum('rhd,nhd->hrn', joined_query, joined_key, preferred_element_ty...]
    all_gather x4 -> x0, local copies, waits for them, and re-layouts: 34.9 us -> none  [the longest x1 8.76 us: on_device(): lax.all_gather(key_loc, 'ctx', axis=0, tiled=True)]
    reshape x8 -> x0, local copies, waits for them, and re-layouts: 34.6 us -> none  [the longest x4 34.5 us: split_heads(): return tensor.reshape(tensor.shape[0], head_count, HD)]
    all_to_all x4 -> x0, waiting for transfers between devices: 28.2 us -> none  [the longest x1 7.68 us: on_device(): lax.all_to_all(d_queries, 'head', split_axis=1, concat_axis=0, tiled=True)]
  transfers between devices with their start and end apart: 8 -> 0, of which waited for: 8 -> 0; matrix products, arithmetic and copies ran while one was open for 5% -> 0% of each run, Pallas kernels for 0% -> 0%
where the time goes in v1:
time: 78.9 us; the launch traced here: 78.6 us
  Pallas kernels  71.4 us (90%)
  local copies, waits for them, and re-layouts  6.63 us (8%)
    pallas_call x1, Pallas kernels, on_device(): pl.pallas_call(functools.partial(kernel, dims), out_shape=(shape, shape),...  71.4 us
    unnamed x14, local copies, waits for them, and re-layouts  6.63 us

profile of v1, /device:TPU:1, one launch (start us, length us, event | category | flops | bytes accessed | tf_op | source)
XLA Modules:
  0.0 78.6 jit_solution(2081330389198474799)
XLA Ops:
  0.6 0.0 copy-start
  0.6 0.9 %copy-done = bf16[16,3072]{1,0:T(8,128)(2,1)S(1)} copy-done((bf16[16,3072]{1,0:T(8,128)(2,1)S(1)}, bf16[16,3072]{1,0:T(8,128)(2,1)}, u32[]{:S(2)}) %copy-start) | copy-done | bytes 98328
  1.5 0.0 copy-start.1
  1.5 0.9 %copy-done.1 = bf16[16,3072]{1,0:T(8,128)(2,1)S(1)} copy-done((bf16[16,3072]{1,0:T(8,128)(2,1)S(1)}, bf16[16,3072]{1,0:T(8,128)(2,1)}, u32[]{:S(2)}) %copy-start.1) | copy-done | bytes 98328
  2.4 0.0 copy-start.2
  2.4 0.9 %copy-done.2 = bf16[16,3072]{1,0:T(8,128)(2,1)S(1)} copy-done((bf16[16,3072]{1,0:T(8,128)(2,1)S(1)}, bf16[16,3072]{1,0:T(8,128)(2,1)}, u32[]{:S(2)}) %copy-start.2) | copy-done | bytes 98328
  3.3 0.0 copy-start.3
  3.3 0.9 %copy-done.3 = bf16[16,3072]{1,0:T(8,128)(2,1)S(1)} copy-done((bf16[16,3072]{1,0:T(8,128)(2,1)S(1)}, bf16[16,3072]{1,0:T(8,128)(2,1)}, u32[]{:S(2)}) %copy-start.3) | copy-done | bytes 98328
  4.2 0.0 copy-start.4
  4.2 0.9 %copy-done.4 = bf16[16,3072]{1,0:T(8,128)(2,1)S(1)} copy-done((bf16[16,3072]{1,0:T(8,128)(2,1)S(1)}, bf16[16,3072]{1,0:T(8,128)(2,1)}, u32[]{:S(2)}) %copy-start.4) | copy-done | bytes 98328
  5.1 0.0 copy-start.5
  5.1 0.9 %copy-done.5 = bf16[16,3072]{1,0:T(8,128)(2,1)S(1)} copy-done((bf16[16,3072]{1,0:T(8,128)(2,1)S(1)}, bf16[16,3072]{1,0:T(8,128)(2,1)}, u32[]{:S(2)}) %copy-start.5) | copy-done | bytes 98328
  6.0 71.4 %shard_map.77 = (bf16[16,3072]{1,0:T(8,128)(2,1)S(1)}, bf16[16,3072]{1,0:T(8,128)(2,1)S(1)}) custom-call(bf16[16,3072]{1,0:T(8,128)(2,1)S(1)} %copy-done, bf16[16,3072]{1,0:T(8,128)(2,1)S(1)} %copy-done.1, bf16[16,3072]{1,0:T(8,128)(2,1)S(1)} %copy-done.2, bf16[16,3072]{1,0:T(8,128)(2,1)S(1)} %copy-done.3, bf16[16,3072]{1,0:T(8,128)(2,1)S(1)} %copy-done.4, ...), custom_call_target="tpu_custom_call" | custom-call | flops 5000000000 | bytes 1000000 | tf_op jit(solution)/shard_map/pallas_call | solution.py:313
  77.4 0.6 copy.10
  78.0 0.6 copy.11
Async XLA Ops:
  0.6 0.9 %copy-start = (bf16[16,3072]{1,0:T(8,128)(2,1)S(1)}, bf16[16,3072]{1,0:T(8,128)(2,1)}, u32[]{:S(2)}) copy-start(bf16[16,3072]{1,0:T(8,128)(2,1)} %q_ref.1) | copy-start | bytes 294916
  1.5 0.9 %copy-start.1 = (bf16[16,3072]{1,0:T(8,128)(2,1)S(1)}, bf16[16,3072]{1,0:T(8,128)(2,1)}, u32[]{:S(2)}) copy-start(bf16[16,3072]{1,0:T(8,128)(2,1)} %k_ref.1) | copy-start | bytes 294916
  2.4 0.9 %copy-start.2 = (bf16[16,3072]{1,0:T(8,128)(2,1)S(1)}, bf16[16,3072]{1,0:T(8,128)(2,1)}, u32[]{:S(2)}) copy-start(bf16[16,3072]{1,0:T(8,128)(2,1)} %v_ref.1) | copy-start | bytes 294916
  3.3 0.9 %copy-start.3 = (bf16[16,3072]{1,0:T(8,128)(2,1)S(1)}, bf16[16,3072]{1,0:T(8,128)(2,1)}, u32[]{:S(2)}) copy-start(bf16[16,3072]{1,0:T(8,128)(2,1)} %dq_ref.1) | copy-start | bytes 294916
  4.2 0.9 %copy-start.4 = (bf16[16,3072]{1,0:T(8,128)(2,1)S(1)}, bf16[16,3072]{1,0:T(8,128)(2,1)}, u32[]{:S(2)}) copy-start(bf16[16,3072]{1,0:T(8,128)(2,1)} %dk_ref.1) | copy-start | bytes 294916
  5.1 0.9 %copy-start.5 = (bf16[16,3072]{1,0:T(8,128)(2,1)S(1)}, bf16[16,3072]{1,0:T(8,128)(2,1)}, u32[]{:S(2)}) copy-start(bf16[16,3072]{1,0:T(8,128)(2,1)} %dv_ref.1) | copy-start | bytes 294916

commit v2 on v1

v2 whole, which is shorter than its diff:
```python
import functools

import jax
import jax.numpy as jnp
import numpy as np
from jax import lax
from jax.experimental import pallas as pl
from jax.experimental.pallas import tpu as pltpu
from jax.sharding import PartitionSpec as P

HD = 128
CORES = 2
SCALE = HD**-0.5
LOG2E = 1.4426950408889634
MESH = pl.DeviceIdType.MESH

DIMS = (4, 8, 8, 2)

PLANS = ("y", "z", "y")


def head_of(slot, place, dims):
    if slot == 1:
        return 2 * dims[1] + place
    return 2 * place + slot // 2


def kernel(
    dims,
    q_ref, k_ref, v_ref, dq_ref, dk_ref, dv_ref,
    out_ref, dout_ref,
    loaded, stage, landed, kb, qb, part, stat, rpart, rstat, outgo, outcome, peak_s, total_s, mean_s, acc_s,
    in_sem, a_send, a_recv, ring_send, ring_recv, sib_send, sib_recv, q_send, q_recv,
    p_send, p_recv, t_send, t_recv, o_send, o_recv,
):
    nx, ny, nz, zlo = dims
    tok = q_ref.shape[0]
    head, ctx = lax.axis_index("head"), lax.axis_index("ctx")
    core = head % CORES
    z = (head // CORES) * zlo + ctx // (ny * nx)
    y = (ctx // nx) % ny
    x = ctx % nx

    def dev(x, y, z, core):
        return ((z // zlo) * CORES + core, (z % zlo) * (ny * nx) + y * nx + x)

    def a_size(s):
        return ny if PLANS[s] == "y" else nz

    def r_size(s):
        return nz if PLANS[s] == "y" else ny

    def a_me(s):
        return y if PLANS[s] == "y" else z

    def r_me(s):
        return z if PLANS[s] == "y" else y

    def a_dev(s, p):
        return dev(x, p, z, core) if PLANS[s] == "y" else dev(x, y, p, core)

    def r_dev(s, r):
        return dev(x, y, r, core) if PLANS[s] == "y" else dev(x, r, z, core)

    sibling = dev(x, y, z, 1 - core)
    rows = nx * 128

    def remote(src, dst, ssem, rsem, to):
        return pltpu.make_async_remote_copy(
            src_ref=src, dst_ref=dst, send_sem=ssem, recv_sem=rsem,
            device_id=to, device_id_type=MESH,
        )

    def drain(ref, sem):
        pltpu.make_async_copy(ref, ref, sem).wait()

    inputs = (k_ref, dk_ref, v_ref, dv_ref, q_ref, dq_ref)
    fetches = [pltpu.make_async_copy(ref, loaded.at[i], in_sem.at[i]) for i, ref in enumerate(inputs)]
    for fetch in fetches:
        fetch.start()

    barrier = pltpu.get_barrier_semaphore()
    peers = [sibling]
    peers += [dev(x, (y + d) % ny, z, core) for d in range(1, ny)]
    peers += [dev(x, y, (z + d) % nz, core) for d in range(1, nz)]
    peers += [dev((x + d) % nx, y, z, core) for d in range(1, nx)]
    for peer in peers:
        pl.semaphore_signal(barrier, inc=1, device_id=peer, device_id_type=MESH)

    for fetch in fetches:
        fetch.wait()
    for s in range(3):
        for p in range(a_size(s)):
            h = head_of(s, p, dims)
            for i in range(6):
                stage[s, p, i] = loaded[i, :, h * HD : (h + 1) * HD]
    pl.semaphore_wait(barrier, len(peers))

    parts = (pl.ds(0, 4), pl.ds(4, 2))

    def scatter(s, i):
        n, me = a_size(s), a_me(s)
        for d in sorted(range(1, n), key=lambda d: -min(d, n - d)):
            p = (me + d) % n
            src, dst = stage.at[s, p, parts[i]], landed.at[s, me, parts[i]]
            remote(src, dst, a_send.at[s, i], a_recv.at[s, i], a_dev(s, p)).start()

    def ring_copy(s, way, r, hops, to):
        block, sem = kb.at[s, core, r], ring_recv.at[s, r]
        if hops == r_size(s) // 2:
            block = block.at[pl.ds(0 if way == 1 else 2, 2)]
            sem = sem if way == 1 else ring_recv.at[s, r_size(s)]
        return remote(block, block, ring_send.at[s], sem, to)

    def sib_copy(s, r, h):
        block = kb.at[s, core, r]
        return remote(block, block, sib_send.at[s], sib_recv.at[s, h], sibling)

    def land(s):
        n, me, r = a_size(s), a_me(s), r_me(s)
        landed[s, me] = stage[s, me]
        if n > 1:
            drain(landed.at[s, pl.ds(0, n - 1), parts[0]], a_recv.at[s, 0])
        for i in range(4):
            for p in range(n):
                kb[s, core, r, i, p * tok : (p + 1) * tok] = landed[s, p, i]

    def ask(s):
        n = a_size(s)
        if n > 1:
            drain(landed.at[s, pl.ds(0, n - 1), parts[1]], a_recv.at[s, 1])
        for i in range(2):
            for p in range(n):
                qb[s, x, i, p * tok : (p + 1) * tok] = landed[s, p, 4 + i]
        for d in range(1, nx):
            mine = qb.at[s, x]
            remote(mine, mine, q_send.at[s], q_recv.at[s], dev((x + d) % nx, y, z, core)).start()

    def begin(s):
        rn, r = r_size(s), r_me(s)
        for way in (1, -1):
            ring_copy(s, way, r, 1, r_dev(s, (r + way) % rn)).start()
        sib_copy(s, r, 0).start()

    def hop(s, h):
        rn, r = r_size(s), r_me(s)
        for way in (1, -1):
            at = (r - way * h) % rn
            ring_copy(s, way, at, h, r_dev(s, r)).wait_recv()
            if h < rn // 2:
                ring_copy(s, way, at, h + 1, r_dev(s, (r + way) % rn)).start()
                sib_copy(s, at, h).start()
        if h == rn // 2:
            sib_copy(s, (r + h) % rn, h).start()

    def attend(s, h):
        rn, r = r_size(s), r_me(s)
        places = [(r + h) % rn, (r - h) % rn][: 1 if h in (0, rn // 2) else 2]
        if h == 0 and nx > 1:
            drain(qb.at[s, pl.ds(0, nx - 1)], q_recv.at[s])
        drain(kb.at[s, 0, pl.ds(0, len(places))], sib_recv.at[s, h])

        def block(i):
            return jnp.concatenate([kb[s, c, at, i] for at in places for c in range(CORES)], axis=0)

        k, dk, v, dv = block(0), block(1), block(2), block(3)
        q = qb[s, :, 0].reshape(rows, HD)
        dq = qb[s, :, 1].reshape(rows, HD)
        nt = (((1,), (1,)), ((), ()))
        score = lax.dot_general(q, k, nt, preferred_element_type=jnp.float32)
        d_score = lax.dot_general(
            jnp.concatenate([dq, q], axis=1), jnp.concatenate([k, dk], axis=1), nt,
            preferred_element_type=jnp.float32,
        )
        peak = jnp.max(score, axis=1, keepdims=True) * (SCALE * LOG2E)
        if h:
            old = peak_s[s, :, :1]
            peak = jnp.maximum(peak, old)
            fade = jnp.exp2(old - peak)
        w = jnp.exp2(score * (SCALE * LOG2E) - peak)
        mix = w * d_score

        def lanes(t):
            return functools.reduce(jnp.add, [t[:, i : i + 128] for i in range(0, t.shape[1], 128)])

        total, mean = lanes(w), lanes(mix)
        both = jnp.dot(
            w.astype(jnp.bfloat16), jnp.concatenate([v, dv], axis=1), preferred_element_type=jnp.float32
        )
        mixed = jnp.dot(mix.astype(jnp.bfloat16), v, preferred_element_type=jnp.float32)
        if h:
            total += total_s[s] * fade
            mean += mean_s[s] * fade
            both += acc_s[s, :, : 2 * HD] * fade
            mixed += acc_s[s, :, 2 * HD :] * fade
        if h < rn // 2:
            peak_s[s] = jnp.broadcast_to(peak, (rows, 128))
            total_s[s] = total
            mean_s[s] = mean
            acc_s[s, :, : 2 * HD] = both
            acc_s[s, :, 2 * HD :] = mixed
            return
        total = jnp.sum(total, axis=1, keepdims=True)
        inv = 1.0 / total
        mean = jnp.sum(mean, axis=1, keepdims=True) * (SCALE * inv)
        primal = both[:, :HD] * inv
        tangent = (mixed * SCALE + both[:, HD:]) * inv - primal * mean
        lane = lax.broadcasted_iota(jnp.int32, (128, 128), 1)
        for c in range(nx):
            rs = slice(c * 128, (c + 1) * 128)
            part[s, c, 0] = primal[rs].astype(jnp.bfloat16)
            part[s, c, 1] = tangent[rs].astype(jnp.bfloat16)
            wide = jnp.where(lane == 0, peak[rs], jnp.where(lane == 1, total[rs], mean[rs]))
            stat[s, c] = wide.T[:8]

    def share(s):
        for d in range(1, nx):
            to = (x + d) % nx
            dst = dev(to, y, z, core)
            remote(part.at[s, to], rpart.at[s, x], p_send.at[s], p_recv.at[s], dst).start()
            remote(stat.at[s, to], rstat.at[s, x], t_send.at[s], t_recv.at[s], dst).start()

    def merge(s):
        rpart[s, x] = part[s, x]
        rstat[s, x] = stat[s, x]
        if nx > 1:
            drain(rpart.at[s, pl.ds(0, nx - 1)], p_recv.at[s])
            drain(rstat.at[s, pl.ds(0, nx - 1)], t_recv.at[s])
        stats = [rstat[s, i] for i in range(nx)]
        top = functools.reduce(jnp.maximum, [t[0:1] for t in stats])
        shares = [jnp.exp2(t[0:1] - top) * t[1:2] for t in stats]
        inv = 1.0 / functools.reduce(jnp.add, shares)
        shares = [a * inv for a in shares]
        mean = functools.reduce(jnp.add, [a * t[2:3] for a, t in zip(shares, stats)])
        rows = [a for a in shares] + [a * (t[2:3] - mean) for a, t in zip(shares, stats)]
        rows.append(jnp.zeros((128 - len(rows), 128), jnp.float32))
        cols = jnp.concatenate(rows, axis=0).T
        primal = jnp.zeros((128, HD), jnp.float32)
        tangent = jnp.zeros((128, HD), jnp.float32)
        for i in range(nx):
            o = rpart[s, i, 0].astype(jnp.float32)
            primal += cols[:, i : i + 1] * o
            tangent += cols[:, i : i + 1] * rpart[s, i, 1].astype(jnp.float32) + cols[:, nx + i : nx + i + 1] * o
        primal, tangent = primal.astype(jnp.bfloat16), tangent.astype(jnp.bfloat16)
        n, me = a_size(s), a_me(s)
        for p in range(n):
            outgo[s, p, 0] = primal[p * tok : (p + 1) * tok]
            outgo[s, p, 1] = tangent[p * tok : (p + 1) * tok]
        for d in sorted(range(1, n), key=lambda d: -min(d, n - d)):
            p = (me + d) % n
            remote(outgo.at[s, p], outcome.at[s, me], o_send.at[s], o_recv.at[s], a_dev(s, p)).start()
        outcome[s, me] = outgo[s, me]

    def finish(s):
        n = a_size(s)
        if n > 1:
            drain(outcome.at[s, pl.ds(0, n - 1)], o_recv.at[s])
        for p in range(n):
            h = head_of(s, p, dims)
            out_ref[:, h * HD : (h + 1) * HD] = outcome[s, p, 0]
            dout_ref[:, h * HD : (h + 1) * HD] = outcome[s, p, 1]

    far = r_size(0) // 2
    scatter(0, 0)
    scatter(1, 0)
    scatter(0, 1)
    scatter(1, 1)
    for s in range(2):
        land(s)
        begin(s)
    scatter(2, 0)
    scatter(2, 1)
    ask(0)
    ask(1)
    for h in range(1, far + 1):
        hop(0, h)
        hop(1, h)
        if h == 1:
            land(2)
            begin(2)
            ask(2)
        attend(0, h - 1)
        if h == far:
            attend(0, h)
            share(0)
        if h > 1:
            hop(2, h - 1)
        attend(1, h - 1)
        if h == far:
            attend(1, h)
            share(1)
        if h > 1:
            attend(2, h - 2)
    hop(2, far)
    attend(2, far - 1)
    merge(0)
    attend(2, far)
    share(2)
    merge(1)
    merge(2)
    for s in range(3):
        finish(s)

    for s in range(3):
        n, rn = a_size(s), r_size(s)
        if n > 1:
            for i in range(2):
                drain(stage.at[s, pl.ds(0, n - 1), parts[i]], a_send.at[s, i])
            drain(outgo.at[s, pl.ds(0, n - 1)], o_send.at[s])
        drain(kb.at[s, 0, pl.ds(0, rn)], sib_send.at[s])
        drain(kb.at[s, 0, pl.ds(0, rn - 1)], ring_send.at[s])
        if nx > 1:
            drain(qb.at[s, pl.ds(0, nx - 1)], q_send.at[s])
            drain(part.at[s, pl.ds(0, nx - 1)], p_send.at[s])
            drain(stat.at[s, pl.ds(0, nx - 1)], t_send.at[s])


def on_device(dims, *arrays):
    nx, ny, nz, _ = dims
    tok = arrays[0].shape[0]
    na = nr = max(ny, nz)
    bf, f32 = jnp.bfloat16, jnp.float32
    dma = pltpu.SemaphoreType.DMA
    shape = jax.ShapeDtypeStruct(arrays[0].shape, bf)
    return pl.pallas_call(
        functools.partial(kernel, dims),
        out_shape=(shape, shape),
        in_specs=[pl.BlockSpec(memory_space=pltpu.HBM)] * 6,
        out_specs=(pl.BlockSpec(memory_space=pltpu.VMEM),) * 2,
        scratch_shapes=[
            pltpu.VMEM((6,) + arrays[0].shape, bf),
            pltpu.VMEM((3, na, 6, tok, HD), bf),
            pltpu.VMEM((3, na, 6, tok, HD), bf),
            pltpu.VMEM((3, CORES, nr, 4, na * tok, HD), bf),
            pltpu.VMEM((3, nx, 2, na * tok, HD), bf),
            pltpu.VMEM((3, nx, 2, 128, HD), bf),
            pltpu.VMEM((3, nx, 8, 128), f32),
            pltpu.VMEM((3, nx, 2, 128, HD), bf),
            pltpu.VMEM((3, nx, 8, 128), f32),
            pltpu.VMEM((3, na, 2, tok, HD), bf),
            pltpu.VMEM((3, na, 2, tok, HD), bf),
            pltpu.VMEM((3, nx * 128, 128), f32),
            pltpu.VMEM((3, nx * 128, 128), f32),
            pltpu.VMEM((3, nx * 128, 128), f32),
            pltpu.VMEM((3, nx * 128, 3 * HD), f32),
            dma((6,)),
            dma((3, 2)), dma((3, 2)),
            dma((3,)), dma((3, nr + 1)),
            dma((3,)), dma((3, nr // 2 + 1)),
            dma((3,)), dma((3,)),
            dma((3,)), dma((3,)),
            dma((3,)), dma((3,)),
            dma((3,)), dma((3,)),
        ],
        compiler_params=pltpu.CompilerParams(
            collective_id=0, has_side_effects=True, vmem_limit_bytes=62 * 1024 * 1024
        ),
        cost_estimate=pl.CostEstimate(flops=5 * 10**9, bytes_accessed=10**6, transcendentals=3 * 10**6),
    )(*arrays)


def solution(mesh):
    spec = P(("head", "ctx"), None)
    return jax.shard_map(
        functools.partial(on_device, DIMS),
        mesh=mesh,
        in_specs=(spec,) * 6,
        out_specs=(spec, spec),
        check_vma=False,
    )
```

time: 78.9 us -> 67.5 us (0.86)
  Pallas kernels: 71.4 us -> 64.2 us
  local copies, waits for them, and re-layouts: 6.63 us -> 2.22 us
    pallas_call x1, Pallas kernels: 71.4 us -> 64.2 us  [on_device(): pl.pallas_call(functools.partial(kernel, dims), out_shape=(shape, shape),...]
    unnamed x14 -> x4, local copies, waits for them, and re-layouts: 6.63 us -> 2.22 us
where the time goes in v2:
time: 67.5 us; the launch traced here: 67.1 us
  Pallas kernels  64.2 us (95%)
  local copies, waits for them, and re-layouts  2.22 us (3%)
    pallas_call x1, Pallas kernels, on_device(): pl.pallas_call(functools.partial(kernel, dims), out_shape=(shape, shape),...  64.2 us
    unnamed x4, local copies, waits for them, and re-layouts  2.22 us

profile of v2, /device:TPU:1, one launch (start us, length us, event | category | flops | bytes accessed | tf_op | source)
XLA Modules:
  0.0 67.1 jit_solution(18257916171515800390)
XLA Ops:
  0.6 64.2 %shard_map.77 = (bf16[16,3072]{1,0:T(8,128)(2,1)}, bf16[16,3072]{1,0:T(8,128)(2,1)}) custom-call(bf16[16,3072]{1,0:T(8,128)(2,1)} %q_ref.1, bf16[16,3072]{1,0:T(8,128)(2,1)} %k_ref.1, bf16[16,3072]{1,0:T(8,128)(2,1)} %v_ref.1, bf16[16,3072]{1,0:T(8,128)(2,1)} %dq_ref.1, bf16[16,3072]{1,0:T(8,128)(2,1)} %dk_ref.1, bf16[16,3072]{1,0:T(8,128)(2,1)} %dv_ref.1), custom_call_target="tpu_custom_call" | custom-call | flops 5000000000 | bytes 1000000 | tf_op jit(solution)/shard_map/pallas_call | solution.py:325
  64.8 0.0 copy-start
  64.9 1.6 %copy.10 = bf16[16,3072]{1,0:T(8,128)(2,1)} copy(bf16[16,3072]{1,0:T(8,128)(2,1)} %get-tuple-element.4) | data formatting | bytes 196608
  66.4 0.0 copy-done
  66.4 0.6 copy.11
Async XLA Ops:
  64.8 1.6 %copy-start = (bf16[16,3072]{1,0:T(8,128)(2,1)S(1)}, bf16[16,3072]{1,0:T(8,128)(2,1)}, u32[]{:S(2)}) copy-start(bf16[16,3072]{1,0:T(8,128)(2,1)} %get-tuple-element.5) | copy-start | bytes 294916

commit v3 on v2

--- a/solution.py
+++ b/solution.py
@@ -293,9 +293,9 @@
             attend(2, h - 2)
     hop(2, far)
     attend(2, far - 1)
-    merge(0)
     attend(2, far)
     share(2)
+    merge(0)
     merge(1)
     merge(2)
     for s in range(3):
@@ -353,10 +353,10 @@
             dma((3,)), dma((3,)),
         ],
         compiler_params=pltpu.CompilerParams(
-            collective_id=0, has_side_effects=True, vmem_limit_bytes=62 * 1024 * 1024
+            collective_id=0, has_side_effects=True, vmem_limit_bytes=40 * 1024 * 1024
         ),
         cost_estimate=pl.CostEstimate(flops=5 * 10**9, bytes_accessed=10**6, transcendentals=3 * 10**6),
-    )(*arrays)
+    )(*[pltpu.with_memory_space_constraint(array, pltpu.HBM) for array in arrays])
 
 
 def solution(mesh):

time: 67.5 us -> 66 us (0.978)
  local copies, waits for them, and re-layouts: 2.22 us -> 1.28 us
    unnamed x4 -> x2, local copies, waits for them, and re-layouts: 2.22 us -> 1.28 us
where the time goes in v3:
time: 66 us; the launch traced here: 65.8 us
  Pallas kernels  63.9 us (97%)
  local copies, waits for them, and re-layouts  1.28 us (2%)
    pallas_call x1, Pallas kernels, on_device(): pl.pallas_call(functools.partial(kernel, dims), out_shape=(shape, shape),...  63.9 us

profile of v3, /device:TPU:1, one launch (start us, length us, event | category | flops | bytes accessed | tf_op | source)
XLA Modules:
  0.0 65.8 jit_solution(9950768685599463825)
XLA Ops:
  0.6 63.9 %shard_map.77 = (bf16[16,3072]{1,0:T(8,128)(2,1)S(1)}, bf16[16,3072]{1,0:T(8,128)(2,1)S(1)}) custom-call(bf16[16,3072]{1,0:T(8,128)(2,1)} %q_ref.1, bf16[16,3072]{1,0:T(8,128)(2,1)} %k_ref.1, bf16[16,3072]{1,0:T(8,128)(2,1)} %v_ref.1, bf16[16,3072]{1,0:T(8,128)(2,1)} %dq_ref.1, bf16[16,3072]{1,0:T(8,128)(2,1)} %dk_ref.1, bf16[16,3072]{1,0:T(8,128)(2,1)} %dv_ref.1), custom_call_target="tpu_custom_call" | custom-call | flops 5000000000 | bytes 1000000 | tf_op jit(solution)/shard_map/pallas_call | solution.py:325
  64.5 0.6 copy.10
  65.2 0.6 copy.11

commit v4 on v3

--- a/solution.py
+++ b/solution.py
@@ -144,6 +144,8 @@
 
     def hop(s, h):
         rn, r = r_size(s), r_me(s)
+        if h > rn // 2:
+            return
         for way in (1, -1):
             at = (r - way * h) % rn
             ring_copy(s, way, at, h, r_dev(s, r)).wait_recv()
@@ -153,12 +155,20 @@
         if h == rn // 2:
             sib_copy(s, (r + h) % rn, h).start()
 
-    def attend(s, h):
+    def attend(s, *levels):
         rn, r = r_size(s), r_me(s)
-        places = [(r + h) % rn, (r - h) % rn][: 1 if h in (0, rn // 2) else 2]
-        if h == 0 and nx > 1:
+        places = []
+        for h in levels:
+            if h > rn // 2:
+                continue
+            found = [(r + h) % rn, (r - h) % rn][: 1 if h in (0, rn // 2) else 2]
+            drain(kb.at[s, 0, pl.ds(0, len(found))], sib_recv.at[s, h])
+            places += found
+        first, final = 0 in levels, rn // 2 in levels
+        if not places:
+            return
+        if first and nx > 1:
             drain(qb.at[s, pl.ds(0, nx - 1)], q_recv.at[s])
-        drain(kb.at[s, 0, pl.ds(0, len(places))], sib_recv.at[s, h])
 
         def block(i):
             return jnp.concatenate([kb[s, c, at, i] for at in places for c in range(CORES)], axis=0)
@@ -173,7 +183,7 @@
             preferred_element_type=jnp.float32,
         )
         peak = jnp.max(score, axis=1, keepdims=True) * (SCALE * LOG2E)
-        if h:
+        if not first:
             old = peak_s[s, :, :1]
             peak = jnp.maximum(peak, old)
             fade = jnp.exp2(old - peak)
@@ -188,12 +198,12 @@
             w.astype(jnp.bfloat16), jnp.concatenate([v, dv], axis=1), preferred_element_type=jnp.float32
         )
         mixed = jnp.dot(mix.astype(jnp.bfloat16), v, preferred_element_type=jnp.float32)
-        if h:
+        if not first:
             total += total_s[s] * fade
             mean += mean_s[s] * fade
             both += acc_s[s, :, : 2 * HD] * fade
             mixed += acc_s[s, :, 2 * HD :] * fade
-        if h < rn // 2:
+        if not final:
             peak_s[s] = jnp.broadcast_to(peak, (rows, 128))
             total_s[s] = total
             mean_s[s] = mean
@@ -260,40 +270,45 @@
             out_ref[:, h * HD : (h + 1) * HD] = outcome[s, p, 0]
             dout_ref[:, h * HD : (h + 1) * HD] = outcome[s, p, 1]
 
-    far = r_size(0) // 2
     scatter(0, 0)
     scatter(1, 0)
     scatter(0, 1)
     scatter(1, 1)
-    for s in range(2):
-        land(s)
-        begin(s)
+    land(0)
+    begin(0)
+    land(1)
+    begin(1)
     scatter(2, 0)
     scatter(2, 1)
     ask(0)
     ask(1)
-    for h in range(1, far + 1):
-        hop(0, h)
-        hop(1, h)
-        if h == 1:
-            land(2)
-            begin(2)
-            ask(2)
-        attend(0, h - 1)
-        if h == far:
-            attend(0, h)
-            share(0)
-        if h > 1:
-            hop(2, h - 1)
-        attend(1, h - 1)
-        if h == far:
-            attend(1, h)
-            share(1)
-        if h > 1:
-            attend(2, h - 2)
-    hop(2, far)
-    attend(2, far - 1)
-    attend(2, far)
+    hop(0, 1)
+    hop(1, 1)
+    land(2)
+    begin(2)
+    ask(2)
+    hop(0, 2)
+    hop(1, 2)
+    hop(2, 1)
+    attend(0, 0, 1)
+    attend(1, 0, 1)
+    hop(0, 3)
+    hop(1, 3)
+    hop(2, 2)
+    attend(0, 2)
+    attend(1, 2)
+    attend(2, 0, 1)
+    hop(0, 4)
+    hop(1, 4)
+    hop(2, 3)
+    attend(0, 3, 4)
+    share(0)
+    attend(1, 3, 4)
+    share(1)
+    attend(2, 2)
+    attend(2, 3)
+    hop(2, 4)
+    attend(2, 4)
     share(2)
     merge(0)
     merge(1)

time: 66 us -> 65.1 us (0.986)
  Pallas kernels: 63.9 us -> 63 us
    pallas_call x1, Pallas kernels: 63.9 us -> 63 us  [on_device(): pl.pallas_call(functools.partial(kernel, dims), out_shape=(shape, shape),...]
where the time goes in v4:
time: 65.1 us; the launch traced here: 64.9 us
  Pallas kernels  63 us (97%)
  local copies, waits for them, and re-layouts  1.28 us (2%)
    pallas_call x1, Pallas kernels, on_device(): pl.pallas_call(functools.partial(kernel, dims), out_shape=(shape, shape),...  63 us

profile of v4, /device:TPU:1, one launch (start us, length us, event | category | flops | bytes accessed | tf_op | source)
XLA Modules:
  0.0 64.9 jit_solution(8602820504139136661)
XLA Ops:
  0.6 63.0 %shard_map.77 = (bf16[16,3072]{1,0:T(8,128)(2,1)S(1)}, bf16[16,3072]{1,0:T(8,128)(2,1)S(1)}) custom-call(bf16[16,3072]{1,0:T(8,128)(2,1)} %q_ref.1, bf16[16,3072]{1,0:T(8,128)(2,1)} %k_ref.1, bf16[16,3072]{1,0:T(8,128)(2,1)} %v_ref.1, bf16[16,3072]{1,0:T(8,128)(2,1)} %dq_ref.1, bf16[16,3072]{1,0:T(8,128)(2,1)} %dk_ref.1, bf16[16,3072]{1,0:T(8,128)(2,1)} %dv_ref.1), custom_call_target="tpu_custom_call" | custom-call | flops 5000000000 | bytes 1000000 | tf_op jit(solution)/shard_map/pallas_call | solution.py:340
  63.7 0.6 copy.10
  64.3 0.6 copy.11

commit v5 on v4

--- a/solution.py
+++ b/solution.py
@@ -224,11 +224,11 @@
             stat[s, c] = wide.T[:8]
 
     def share(s):
-        for d in range(1, nx):
+        for d in sorted(range(1, nx), key=lambda d: -min(d, nx - d)):
             to = (x + d) % nx
             dst = dev(to, y, z, core)
+            remote(stat.at[s, to], rstat.at[s, x], t_send.at[s], t_recv.at[s], dst).start()
             remote(part.at[s, to], rpart.at[s, x], p_send.at[s], p_recv.at[s], dst).start()
-            remote(stat.at[s, to], rstat.at[s, x], t_send.at[s], t_recv.at[s], dst).start()
 
     def merge(s):
         rpart[s, x] = part[s, x]

time: 65.1 us -> 64.9 us (level)
  no operation moved by 1% of the time
where the time goes in v5:
time: 64.9 us; the launch traced here: 64.7 us
  Pallas kernels  62.8 us (97%)
  local copies, waits for them, and re-layouts  1.28 us (2%)
    pallas_call x1, Pallas kernels, on_device(): pl.pallas_call(functools.partial(kernel, dims), out_shape=(shape, shape),...  62.8 us

profile of v5, /device:TPU:1, one launch (start us, length us, event | category | flops | bytes accessed | tf_op | source)
XLA Modules:
  0.0 64.7 jit_solution(7544461559161540334)
XLA Ops:
  0.6 62.8 %shard_map.77 = (bf16[16,3072]{1,0:T(8,128)(2,1)S(1)}, bf16[16,3072]{1,0:T(8,128)(2,1)S(1)}) custom-call(bf16[16,3072]{1,0:T(8,128)(2,1)} %q_ref.1, bf16[16,3072]{1,0:T(8,128)(2,1)} %k_ref.1, bf16[16,3072]{1,0:T(8,128)(2,1)} %v_ref.1, bf16[16,3072]{1,0:T(8,128)(2,1)} %dq_ref.1, bf16[16,3072]{1,0:T(8,128)(2,1)} %dk_ref.1, bf16[16,3072]{1,0:T(8,128)(2,1)} %dv_ref.1), custom_call_target="tpu_custom_call" | custom-call | flops 5000000000 | bytes 1000000 | tf_op jit(solution)/shard_map/pallas_call | solution.py:340
  63.4 0.6 copy.10
  64.1 0.6 copy.11
